TPU v7x, 128 devices: a whole 4x4x4 slice. The times are simulated.
128 devices in a mesh: dp: 4 (over z), ctx: 32 (over x, y, core).
Axes of the slice: x: 4, y: 4, z: 4, core: 2. Of those that a mesh axis runs over, the one named last changes fastest.
Arguments:
- byte_query: bfloat16 [4, 8192, 4096], P('dp', 'ctx'), may hold values from -6 to 6
- byte_key_value: bfloat16 [4, 8192, 2048], P('dp', 'ctx'), may hold values from -6 to 6
- out_grads: bfloat16 [4, 8192, 4096], P('dp', 'ctx'), may hold values from -6 to 6
- patch_starts: int32 [4, 2048], P('dp'), may hold values from 0 to 8191, as said below
- query_gain: float32 [128], replicated, may hold values from 0.1 to 1.9
- key_gain: float32 [128], replicated, may hold values from 0.1 to 1.9
Outputs:
- byte_query_grad: bfloat16 [4, 8192, 4096], P('dp', 'ctx')
- byte_keyval_grad: bfloat16 [4, 8192, 2048], P('dp', 'ctx')
- query_gain_grad: float32 [128], replicated
- key_gain_grad: float32 [128], replicated
Inputs may be any that keep to these rules, and one draw needn't show every extreme that they name: `patch_starts`: each row rises strictly and begins with 0. There are integers e_0 to e_(31) in -16 to 16, with e_(31) = 0 and e_(-1) = 0, such that the patches that begin in bytes k * 256 to (k + 1) * 256 - 1 are the patches k * 64 + e_(k - 1) to (k + 1) * 64 + e_k - 1; in every row some e_k is 16 and another is -16.
All inputs are finite; a program needn't handle non-finite values.
Results may differ from a plain program's by a relative error of at most 0.02.
Values may be sent and summed in bfloat16 or wider, within the bound.
No kernel may reach another device: no remote copies, remote signals or barrier semaphores. Data moves between devices by JAX's collectives and lax.ppermute only.
A program may use at most 128 MiB of HBM per device.

v0:
```python
import functools
import math

import jax
import jax.numpy as jnp
from jax import lax
from jax.experimental import pallas as pl
from jax.experimental.pallas import tpu as pltpu
from jax.sharding import PartitionSpec as P

eps_norm = 1e-06
head = 128
below_rows = 32
above_rows = 16
edge = 16
query_blk = 1024
key_blk = 256
extra = 8
f32 = jnp.float32
bf16 = jnp.bfloat16
nt = (((1,), (1,)), ((), ()))


def limit(mib):
    return pltpu.CompilerParams(vmem_limit_bytes=mib * 1024 * 1024)


def folded(row, width):
    pieces = [row[:, at : at + width] for at in range(0, row.shape[1], width)]
    return jnp.concatenate(pieces + [jnp.zeros((edge - len(pieces), width), f32)], axis=0)


def unfolded(block, count):
    return jnp.concatenate([block[n : n + 1] for n in range(count)], axis=1)


def bottom(row):
    at = lax.broadcasted_iota(jnp.int32, (edge, row.shape[1]), 0)
    return jnp.where(at == edge - 1, row, 0.0)


def is_even(shard_ref):
    return lax.rem(shard_ref[0], 2) == 0


def pool_kernel(
    shard_ref,
    starts_ref,
    query_ref,
    keyval_ref,
    grad_ref,
    own_ref,
    rims_ref,
    edges_ref,
    query_buf,
    keyval_buf,
    grad_buf,
    starts_buf,
    sems,
):
    bytes_dev, query_width = query_ref.shape
    half = keyval_ref.shape[1] // 2
    patches = starts_ref.shape[1]
    chunks, own, _ = own_ref.shape
    qcols, kcols = query_width // chunks, half // chunks
    shard = shard_ref[0]
    used = below_rows + own + above_rows

    def parts(c):
        return (
            (query_buf, c * qcols, qcols),
            (grad_buf, c * qcols, qcols),
            (keyval_buf, c * kcols, kcols),
            (keyval_buf, half + c * kcols, kcols),
        )

    def copies(c):
        cols = slice(c * qcols, (c + 1) * qcols)
        pairs = [(query_ref.at[:, cols], query_buf.at[:, cols]), (grad_ref.at[:, cols], grad_buf.at[:, cols])]
        if c == 0:
            pairs = [(keyval_ref, keyval_buf)] + pairs
        return [pltpu.make_async_copy(ref, buf, sems.at[c, n]) for n, (ref, buf) in enumerate(pairs)]

    starts_copy = pltpu.make_async_copy(starts_ref, starts_buf, sems.at[chunks, 0])
    starts_copy.start()
    for c in range(chunks):
        for copy in copies(c):
            copy.start()

    first_patch = shard * own - below_rows
    starts_copy.wait()
    around = jnp.broadcast_to(starts_buf[...], (8, patches))
    around = pltpu.roll(around, lax.rem(patches - first_patch, patches), 1)
    lane = lax.broadcasted_iota(jnp.int32, (1, 128), 1) + first_patch

    def limited(values, at):
        values = jnp.where(at < 0, 0, jnp.where(at >= patches, bytes_dev * (patches // own), values))
        return values - shard * bytes_dev

    start = limited(around[0:1, 0:128], lane)
    end = limited(around[0:1, 1:129], lane + 1)
    edges_ref[0:1, :] = start
    edges_ref[1:2, :] = end
    place = lax.broadcasted_iota(jnp.int32, (bytes_dev, 128), 0)
    inside = jnp.where((start <= place) & (place < end), 1.0, 0.0)
    pick = inside.T.astype(bf16)[:used, :]
    for c in range(chunks):
        for copy in copies(c):
            copy.wait()
        out = 0
        below, above, lone = [], [], []
        for buf, at, width in parts(c):
            sums = jnp.dot(pick, buf[:, at : at + width], preferred_element_type=f32)
            own_ref[c, :, out : out + width] = sums[below_rows : below_rows + own]
            lone.append(sums[edge - 1 : edge])
            below.append(sums[edge:below_rows])
            above.append(sums[below_rows + own :])
            out += width
        lone = folded(jnp.concatenate(lone, axis=1), 2 * head)
        rims_ref[c, :edge, :] = jnp.concatenate(below + [lone], axis=1).astype(bf16)
        rims_ref[c, edge:, :] = jnp.concatenate(above + [jnp.zeros_like(lone)], axis=1).astype(bf16)


def rimmed(rows, early, lone, late):
    gap = jnp.zeros((rows.shape[0] - 3 * edge, rows.shape[1]), f32)
    return rows + jnp.concatenate([early, gap, bottom(lone), late], axis=0)


def send_kernel(shard_ref, own_ref, rims_ref, send_ref):
    chunks, own, width = own_ref.shape
    heads = 2 * send_ref.shape[0] // chunks
    groups = (width // head - 2 * heads) // 2
    even = is_even(shard_ref)

    def chunk(c, carry):
        got = rims_ref[c].astype(f32)
        below, above, lone = got[:edge, :width], got[edge:, :width], unfolded(got[:edge, width:], width // (2 * head))
        early, late = jnp.where(even, 0.0, above), jnp.where(even, below, 0.0)
        far, far_lone = jnp.where(even, above, below), jnp.where(even, 0.0, lone)
        lone = jnp.where(even, lone, 0.0)

        def put(chip, part, tile):
            cols = slice(tile * head, (tile + 1) * head)
            rows = rimmed(own_ref[c, :, cols], early[:, cols], lone[:, cols], late[:, cols])
            send_ref[chip, part * own : (part + 1) * own, :] = rows.astype(bf16)
            at = 6 * own + part * edge
            send_ref[chip, at : at + edge, :] = far[:, cols].astype(bf16)
            return far_lone[:, cols]

        for n in range(heads // 2):
            chip = c * heads // 2 + n
            group = n * groups // (heads // 2)
            tiles = [2 * n, 2 * n + 1, heads + 2 * n, heads + 2 * n + 1, 2 * heads + group, 2 * heads + groups + group]
            ends = [put(chip, part, tile) for part, tile in enumerate(tiles)]
            ends = jnp.concatenate(ends + [jnp.zeros((extra - 6, head), f32)], axis=0)
            send_ref[chip, 6 * (own + edge) :, :] = ends.astype(bf16)
        return carry

    lax.fori_loop(0, chunks, chunk, 0)


def summed_part(mine_ref, even, c, part, own):
    chips = mine_ref.shape[0]
    at = 6 * own + part * edge
    none = jnp.zeros((edge, head), f32)
    early = late = none
    lone = none[:1]
    if c > 0:
        early = jnp.where(even, mine_ref[c - 1, at : at + edge, :].astype(f32), 0.0)
    if c < chips - 1:
        late = jnp.where(even, 0.0, mine_ref[c + 1, at : at + edge, :].astype(f32))
        lone = mine_ref[c + 1, 6 * (own + edge) :, :].astype(f32)[part : part + 1]
        lone = jnp.where(even, 0.0, lone)
    return rimmed(mine_ref[c, part * own : (part + 1) * own, :].astype(f32), early, lone, late)


def inverse_rms(rows):
    return lax.rsqrt(jnp.mean(rows * rows, axis=-1, keepdims=True) + eps_norm)


def lengths_kernel(shard_ref, starts_ref, inv_ref, *, document):
    chips, own, _ = inv_ref.shape
    lanes = starts_ref.shape[1] // chips
    starts = starts_ref[...].astype(f32)
    ends = jnp.concatenate([starts[:, 1:], jnp.full((1, 1), document, f32)], axis=1)
    lengths = ends - starts
    table = jnp.concatenate([lengths[:, c * lanes : (c + 1) * lanes] for c in range(chips)], axis=0)
    table = 1.0 / table.T
    table = jnp.where(is_even(shard_ref), table[:own], table[own:])
    for c in range(chips):
        inv_ref[c] = jnp.broadcast_to(table[:, c : c + 1], (own, head))


def keys_kernel(shard_ref, mine_ref, inv_ref, kgain_ref, keyval_ref, mean_ref):
    chips, own, _ = inv_ref.shape
    even = is_even(shard_ref)
    for c in range(chips):
        inv_len = inv_ref[c]
        rows = summed_part(mine_ref, even, c, 4, own) * inv_len
        mean_ref[c] = rows
        keyval_ref[c, :own, :] = (rows * inverse_rms(rows) * kgain_ref[...]).astype(bf16)
        keyval_ref[c, own:, :] = (summed_part(mine_ref, even, c, 5, own) * inv_len).astype(bf16)


def queries_kernel(shard_ref, mine_ref, inv_ref, qgain_ref, query_ref, grad_ref, unit_ref, scale_ref):
    chips, own, _ = inv_ref.shape
    even = is_even(shard_ref)
    for c in range(chips):
        for n in range(2):
            at = slice(n * own, (n + 1) * own)
            rows = summed_part(mine_ref, even, c, n, own) * inv_ref[c]
            inverse = inverse_rms(rows)
            unit = rows * inverse
            unit_ref[c, at, :] = unit
            scale_ref[c, at, :] = inverse * inv_ref[c]
            query_ref[c, at, :] = (unit * qgain_ref[...]).astype(bf16)
            grad_ref[c, at, :] = summed_part(mine_ref, even, c, 2 + n, own).astype(bf16)


def attend_kernel(
    shard_ref,
    query_ref,
    grad_ref,
    mine_ref,
    other_ref,
    qgain_ref,
    kgain_ref,
    dq_ref,
    keep_ref,
    give_ref,
    gain_ref,
    key_ref,
    value_ref,
    keyt_ref,
    raised0_ref,
    raised1_ref,
    dw0_ref,
    dw1_ref,
    dk_ref,
    dv_ref,
    dqt_ref,
):
    chips, own = mine_ref.shape[0], mine_ref.shape[1] // 2
    patches = key_ref.shape[0]
    per = query_blk // key_blk
    count = patches // query_blk
    lanes = 2 * own
    scaling = head ** (-0.5)
    raising = scaling * math.log2(math.e)
    raised_refs, dw_refs = (raised0_ref, raised1_ref), (dw0_ref, dw1_ref)
    side = lax.rem(shard_ref[0], 2)

    def places(c):
        mine = pl.multiple_of(c * lanes + side * own, own)
        theirs = pl.multiple_of(c * lanes + (1 - side) * own, own)
        return pl.ds(mine, own), pl.ds(theirs, own)

    for c in range(chips):
        mine, theirs = places(c)
        key_ref[mine, :] = mine_ref[c, :own, :]
        value_ref[mine, :] = mine_ref[c, own:, :]
        key_ref[theirs, :] = other_ref[c, :own, :]
        value_ref[theirs, :] = other_ref[c, own:, :]

    for n in range(patches // key_blk):
        keyt_ref[n] = key_ref[pl.ds(n * key_blk, key_blk), :].astype(f32).T.astype(bf16)
    dk_ref[...] = jnp.zeros_like(dk_ref)
    dv_ref[...] = jnp.zeros_like(dv_ref)

    def fold(block):
        return jnp.sum(block.reshape(block.shape[0] // 8, 8, block.shape[1]), axis=0)

    def rows(i, lane, part):
        first_chip, last_chip = (i * query_blk + lane) // lanes, (i + 1) * query_blk // lanes
        block = (query_ref, grad_ref)[part][first_chip:last_chip]
        return block.reshape(query_blk - lane, head)

    def first(i, at, lane, sums, diagonal):
        keys = pl.ds(at, key_blk)
        scores = lax.dot_general(key_ref[keys, :], rows(i, lane, 0), nt, preferred_element_type=f32)
        raised = jnp.exp2(scores * raising)
        if diagonal:
            key_at = lax.broadcasted_iota(jnp.int32, raised.shape, 0)
            query_at = lax.broadcasted_iota(jnp.int32, raised.shape, 1)
            query_at = query_at - lax.bitwise_and(query_at, own) + side * own
            raised = jnp.where(key_at <= query_at, raised, 0.0)
        dweights = lax.dot_general(value_ref[keys, :], rows(i, lane, 1), nt, preferred_element_type=f32)
        raised_refs[i % 2][keys, lane:] = raised
        dw_refs[i % 2][keys, lane:] = dweights
        added = fold(raised), fold(raised * dweights)
        if lane:
            none = jnp.zeros((8, lane), f32)
            added = tuple(jnp.concatenate([none, x], axis=1) for x in added)
        return (sums[0] + added[0], sums[1] + added[1])

    def second(i, at, lane, stats):
        keys = pl.ds(at, key_blk)
        inv_sum, delta = stats[0][:, lane:], stats[1][:, lane:]
        weights = raised_refs[i % 2][keys, lane:] * inv_sum
        dscores = (weights * (dw_refs[i % 2][keys, lane:] - delta)).astype(bf16)
        dv_ref[keys, :] += jnp.dot(weights.astype(bf16), rows(i, lane, 1), preferred_element_type=f32)
        dk_ref[keys, :] += jnp.dot(dscores, rows(i, lane, 0), preferred_element_type=f32)
        n = at // key_blk if isinstance(at, int) else lax.div(at, key_blk)
        dqt_ref[:, lane:] += jnp.dot(keyt_ref[n], dscores, preferred_element_type=f32)

    zero = jnp.zeros((8, query_blk), f32)
    total = jnp.zeros((1, head), f32)
    stats = None
    for i in range(count + 1):
        sums = (zero, zero)
        if i > 0:
            dqt_ref[...] = jnp.zeros_like(dqt_ref)

            def both(j, sums, i=i, stats=stats):
                second(i - 1, j * key_blk, 0, stats)
                return first(i, j * key_blk, 0, sums, False) if i < count else sums

            if i > 1:
                sums = lax.fori_loop(0, (i - 1) * per, both, sums, unroll=2)
            for n in range(per):
                at = (i - 1) * query_blk + n * key_blk
                second(i - 1, at, n * key_blk, stats)
                if i < count:
                    sums = first(i, at, 0, sums, False)
        if i < count:
            for n in range(per):
                sums = first(i, i * query_blk + n * key_blk, n * key_blk, sums, True)
        if i > 0:
            dq = dqt_ref[...].T * scaling
            at = query_blk // lanes
            dq_ref[(i - 1) * at : i * at] = dq.reshape(at, lanes, head)
            total = total + jnp.sum(dq * rows(i - 1, 0, 0).astype(f32), axis=0, keepdims=True)
        if i < count:
            inv_sum = 1.0 / jnp.sum(sums[0], axis=0, keepdims=True)
            stats = (inv_sum, jnp.sum(sums[1], axis=0, keepdims=True) * inv_sum)

    key_total = jnp.zeros((1, head), f32)
    for n in range(patches // key_blk):
        at = pl.ds(n * key_blk, key_blk)
        dk = dk_ref[at, :] * scaling
        dk_ref[at, :] = dk
        key_total = key_total + jnp.sum(dk * key_ref[at, :].astype(f32), axis=0, keepdims=True)

    for c in range(chips):
        mine, theirs = places(c)
        keep_ref[c, :own, :] = dk_ref[mine, :]
        keep_ref[c, own:, :] = dv_ref[mine, :]
        give_ref[c, :own, :] = dk_ref[theirs, :].astype(bf16)
        give_ref[c, own:, :] = dv_ref[theirs, :].astype(bf16)
    gains = jnp.concatenate([total / qgain_ref[...], key_total / kgain_ref[...]], axis=0)
    parts = in_parts(gains)
    gain_ref[...] = parts
    give_ref[chips] = jnp.concatenate([parts, jnp.zeros((lanes - extra, head), f32)], axis=0).astype(bf16)


def in_parts(gains):
    high = gains.astype(bf16).astype(f32)
    middle = (gains - high).astype(bf16).astype(f32)
    low = (gains - high - middle).astype(bf16).astype(f32)
    return jnp.concatenate([high, middle, low, jnp.zeros((extra - 6, head), f32)], axis=0)


def joined(parts):
    return parts[0:2] + parts[2:4] + parts[4:6]


def norm_back(delta, gain, unit, scale):
    scaled = delta * gain
    return scale * (scaled - unit * jnp.mean(scaled * unit, axis=-1, keepdims=True))


def finish_kernel(dq_ref, unit_ref, scale_ref, qgain_ref, kmean_ref, inv_ref, rows_ref, kunit_ref, kscale_ref):
    for c in range(rows_ref.shape[0]):
        rows_ref[c] = norm_back(dq_ref[c], qgain_ref[...], unit_ref[c], scale_ref[c]).astype(bf16)
        mean = kmean_ref[c]
        inverse = inverse_rms(mean)
        kunit_ref[c] = mean * inverse
        kscale_ref[c] = inverse * inv_ref[c]


def merge_kernel(
    shard_ref, rows_ref, keep_ref, got_ref, gain_ref, near_ref, cross_ref, kunit_ref, kscale_ref, inv_ref, kgain_ref, out_ref
):
    chips, own, _ = inv_ref.shape
    even = is_even(shard_ref)
    here = joined(gain_ref[...]) + joined(got_ref[chips].astype(f32))
    tail = in_parts(here + (joined(near_ref[...]) + joined(cross_ref[...])))[:6]
    for c in range(chips):
        kept = keep_ref[c] + got_ref[c].astype(f32)
        keys = norm_back(kept[:own], kgain_ref[...], kunit_ref[c], kscale_ref[c])
        out_ref[c, : 2 * own, :] = rows_ref[c]
        out_ref[c, 2 * own : 3 * own, :] = keys.astype(bf16)
        out_ref[c, 3 * own : 4 * own, :] = (kept[own:] * inv_ref[c]).astype(bf16)
    none = jnp.zeros((edge, head), f32)
    for c in range(chips):
        lones = []
        for part in range(4):
            above = below = lone = none
            if c < chips - 1:
                above = out_ref[c + 1, part * own : part * own + edge, :].astype(f32)
            if c > 0:
                end = (part + 1) * own
                below = out_ref[c - 1, end - edge : end, :].astype(f32)
                lone = out_ref[c - 1, end - 2 * edge : end - edge, :].astype(f32)
            at = 4 * own + part * edge
            out_ref[c, at : at + edge, :] = jnp.where(even, above, below).astype(bf16)
            lones.append(lone[edge - 1 :])
        last = jnp.concatenate([tail] + lones + [none[: edge - 10]], axis=0)
        out_ref[c, 4 * (own + edge) :, :] = last.astype(bf16)


def back_kernel(shard_ref, x_ref, rows_ref, rims_ref, gain_ref):
    chips = x_ref.shape[0]
    chunks, own, width = rows_ref.shape
    per = 2 * chips // chunks
    groups = (width // head - per) * chunks // 2
    repeat = chips // groups
    even = is_even(shard_ref)

    def pieces(chip, part):
        at = 4 * own + part * edge
        ends = x_ref[chip, 4 * (own + edge) :, :].astype(f32)
        return (
            x_ref[chip, part * own : (part + 1) * own, :].astype(f32),
            x_ref[chip, at : at + edge, :].astype(f32),
            ends[6 + part : 7 + part],
        )

    def keyval_pieces(n):
        part, group = n // groups, n % groups
        terms = [pieces(group * repeat + r, 2 + part) for r in range(repeat)]
        return tuple(sum(term[1:], term[0]) for term in zip(*terms))

    tiles = 2 * groups // chunks
    for c in range(chunks):
        parts = [pieces((c * per + n) // 2, n % 2) for n in range(per)]
        parts += [keyval_pieces(c * tiles + n) for n in range(tiles)]
        before, after, lone = [], [], []
        for n, (rows, far, far_lone) in enumerate(parts):
            rows_ref[c, :, n * head : (n + 1) * head] = rows.astype(bf16)
            before.append(jnp.where(even, rows[own - edge :], far))
            after.append(jnp.where(even, far, rows[:edge]))
            lone.append(jnp.where(even, rows[own - edge - 1 : own - edge], far_lone))
        lone = folded(jnp.concatenate(lone, axis=1), head)
        rims_ref[c, :edge, :] = jnp.concatenate(before + [lone], axis=1).astype(bf16)
        rims_ref[c, edge:, :] = jnp.concatenate(after + [jnp.zeros_like(lone)], axis=1).astype(bf16)

    tail = x_ref[0, 4 * (own + edge) :, :].astype(f32)
    for c in range(1, chips):
        tail = tail + x_ref[c, 4 * (own + edge) :, :].astype(f32)
    gain_ref[...] = joined(tail)


def spread_kernel(edges_ref, rims_ref, rows_ref, query_ref, keyval_ref, query_buf, keyval_buf, sems):
    bytes_dev, query_width = query_ref.shape
    chunks, own, width = rows_ref.shape
    qcols, vcols = query_width // chunks, keyval_ref.shape[1] // chunks
    start = edges_ref[0:1, :]
    end = edges_ref[1:2, :]
    place = lax.broadcasted_iota(jnp.int32, (bytes_dev, 128), 0)
    pick = jnp.where((start <= place) & (place < end), 1.0, 0.0).astype(bf16)
    pick = pick[:, : below_rows + own + above_rows]
    running = []
    for c in range(chunks):
        before, after = rims_ref[c, :edge, :].astype(f32), rims_ref[c, edge:, :]
        lone = bottom(unfolded(before[:, width:], width // head))
        early = jnp.concatenate([lone, before[:, :width]], axis=0).astype(bf16)
        rows = jnp.concatenate([early, rows_ref[c], after[:, :width]], axis=0)
        out = jnp.dot(pick, rows, preferred_element_type=f32).astype(bf16)
        query_buf[:, c * qcols : (c + 1) * qcols] = out[:, :qcols]
        keyval_buf[:, c * vcols : (c + 1) * vcols] = out[:, qcols:]
        for n, (buf, ref, cols) in enumerate(((query_buf, query_ref, qcols), (keyval_buf, keyval_ref, vcols))):
            at = c * cols
            copy = pltpu.make_async_copy(buf.at[:, at : at + cols], ref.at[:, at : at + cols], sems.at[c, n])
            copy.start()
            running.append(copy)
    for copy in running:
        copy.wait()


def shards(byte_query, byte_key_value, out_grads, patch_starts, query_gain, key_gain):
    byte_query, byte_key_value, out_grads = byte_query[0], byte_key_value[0], out_grads[0]
    bytes_dev, query_width = byte_query.shape
    keyval_width = byte_key_value.shape[1]
    devices = lax.axis_size("ctx")
    chips = devices // 2
    shard = lax.axis_index("ctx")
    patches = patch_starts.shape[1]
    own = patches // devices
    chunks = 4
    qcols, kcols = query_width // chunks, keyval_width // 2 // chunks
    chunk_cols = 2 * qcols + 2 * kcols

    which = shard.astype(jnp.int32).reshape(1)

    def shape(kind, *dims):
        return jax.ShapeDtypeStruct(dims, kind)

    smem = pl.BlockSpec(memory_space=pltpu.SMEM)
    vmem = pl.BlockSpec(memory_space=pltpu.VMEM)
    hbm = pl.BlockSpec(memory_space=pltpu.HBM)
    mates = [(i, i ^ 1) for i in range(devices)]

    wide = chunk_cols + 2 * head
    inputs = (patch_starts, byte_query, byte_key_value, out_grads)
    sums, rims, edges = pl.pallas_call(
        pool_kernel,
        in_specs=[smem] + [hbm] * 4,
        out_specs=[vmem] * 3,
        out_shape=[
            shape(f32, chunks, own, chunk_cols),
            shape(bf16, chunks, 2 * edge, wide),
            shape(jnp.int32, 2, 128),
        ],
        scratch_shapes=[
            pltpu.VMEM((bytes_dev, query_width), bf16),
            pltpu.VMEM((bytes_dev, keyval_width), bf16),
            pltpu.VMEM((bytes_dev, query_width), bf16),
            pltpu.VMEM((1, patches), jnp.int32),
            pltpu.SemaphoreType.DMA((chunks + 1, 3)),
        ],
        compiler_params=limit(20),
        name="pool",
    )(which, *(pltpu.with_memory_space_constraint(x, pltpu.HBM) for x in inputs))
    rims = lax.ppermute(rims, "ctx", mates)
    inv_len = pl.pallas_call(
        functools.partial(lengths_kernel, document=bytes_dev * devices),
        in_specs=[smem, vmem],
        out_specs=vmem,
        out_shape=shape(f32, chips, own, head),
        compiler_params=limit(16),
        name="lengths",
    )(which, patch_starts)
    rims, inv_len = lax.optimization_barrier((rims, inv_len))

    send = pl.pallas_call(
        send_kernel,
        in_specs=[smem] + [vmem] * 2,
        out_specs=vmem,
        out_shape=shape(bf16, chips, 6 * (own + edge) + extra, head),
        compiler_params=limit(20),
        name="send",
    )(which, sums, rims)

    sides = [list(range(n, devices, 2)) for n in range(2)]
    mine = lax.all_to_all(send, "ctx", 0, 0, tiled=True, axis_index_groups=sides)
    qgain, kgain = query_gain[None], key_gain[None]
    pair = (chips, 2 * own, head)
    keyval, kmean = pl.pallas_call(
        keys_kernel,
        in_specs=[smem] + [vmem] * 3,
        out_specs=[vmem] * 2,
        out_shape=[shape(bf16, *pair), shape(f32, chips, own, head)],
        compiler_params=limit(20),
        name="keys",
    )(which, mine, inv_len, kgain)
    other = lax.ppermute(keyval, "ctx", mates)
    query, grad, qunit, qscale = pl.pallas_call(
        queries_kernel,
        in_specs=[smem] + [vmem] * 3,
        out_specs=[vmem] * 4,
        out_shape=[shape(bf16, *pair), shape(bf16, *pair), shape(f32, *pair), shape(f32, *pair)],
        compiler_params=limit(20),
        name="queries",
    )(which, mine, inv_len, qgain)

    block = (patches, head)
    dq, keep, give, gains = pl.pallas_call(
        attend_kernel,
        in_specs=[smem] + [vmem] * 6,
        out_specs=[vmem] * 4,
        out_shape=[
            shape(f32, *pair),
            shape(f32, *pair),
            shape(bf16, chips + 1, 2 * own, head),
            shape(f32, extra, head),
        ],
        scratch_shapes=[pltpu.VMEM(block, bf16)] * 2
        + [pltpu.VMEM((patches // key_blk, head, key_blk), bf16)]
        + [pltpu.VMEM((patches - query_blk, query_blk), f32), pltpu.VMEM((patches, query_blk), f32)] * 2
        + [pltpu.VMEM(block, f32)] * 2
        + [pltpu.VMEM((head, query_blk), f32)],
        compiler_params=limit(36),
        name="attend",
    )(which, query, grad, keyval, other, qgain, kgain)
    got = lax.ppermute(give, "ctx", mates)
    docs = lax.axis_size("dp")
    near = lax.ppermute(gains, "dp", [(i, i ^ 1) for i in range(docs)])
    crossed = [(d * devices + i, (d ^ 1) * devices + (i ^ 1)) for d in range(docs) for i in range(devices)]
    cross = lax.ppermute(gains, ("dp", "ctx"), crossed)

    rows, kunit, kscale = pl.pallas_call(
        finish_kernel,
        in_specs=[vmem] * 6,
        out_specs=[vmem] * 3,
        out_shape=[shape(bf16, *pair), shape(f32, chips, own, head), shape(f32, chips, own, head)],
        compiler_params=limit(20),
        name="finish",
    )(dq, qunit, qscale, qgain, kmean, inv_len)
    back = pl.pallas_call(
        merge_kernel,
        in_specs=[smem] + [vmem] * 10,
        out_specs=vmem,
        out_shape=shape(bf16, chips, 4 * (own + edge) + edge, head),
        compiler_params=limit(16),
        name="merge",
    )(which, rows, keep, got, gains, near, cross, kunit, kscale, inv_len, kgain)
    home = lax.all_to_all(back, "ctx", 0, 0, tiled=True, axis_index_groups=sides)

    vcols = keyval_width // chunks
    wide = qcols + vcols + head
    rows, rims, gains = pl.pallas_call(
        back_kernel,
        in_specs=[smem, vmem],
        out_specs=[vmem] * 3,
        out_shape=[
            shape(bf16, chunks, own, qcols + vcols),
            shape(bf16, chunks, 2 * edge, wide),
            shape(f32, 2, head),
        ],
        compiler_params=limit(32),
        name="back",
    )(which, home)
    rims = lax.ppermute(rims, "ctx", mates)
    opposite = lax.ppermute(gains, "dp", [(i, docs - 1 - i) for i in range(docs)])
    query_out, keyval_out = pl.pallas_call(
        spread_kernel,
        in_specs=[vmem] * 3,
        out_specs=[hbm] * 2,
        out_shape=[shape(bf16, bytes_dev, query_width), shape(bf16, bytes_dev, keyval_width)],
        scratch_shapes=[
            pltpu.VMEM((bytes_dev, query_width), bf16),
            pltpu.VMEM((bytes_dev, keyval_width), bf16),
            pltpu.SemaphoreType.DMA((chunks, 2)),
        ],
        compiler_params=limit(20),
        name="spread",
    )(edges, rims, rows)
    keyval_out, opposite = lax.optimization_barrier((keyval_out, opposite))
    gains = gains + opposite
    return (query_out[None], keyval_out[None], gains[0], gains[1])


def solution(mesh):
    placed = (
        P("dp", "ctx", None),
        P("dp", "ctx", None),
        P("dp", "ctx", None),
        P("dp", None),
        P(),
        P(),
    )
    return jax.shard_map(
        shards,
        mesh=mesh,
        in_specs=placed,
        out_specs=(P("dp", "ctx", None), P("dp", "ctx", None), P(), P()),
        check_vma=False,
    )
```

profile of v0, /device:TPU:1, one launch (start us, length us, event | category | flops | bytes accessed | tf_op | source)
XLA Modules:
  0.0 87.1 jit_solution(1113029962618347632)
XLA Ops:
  0.6 0.0 copy-start
  0.6 3.1 %pool.1 = (f32[4,64,2560]{2,1,0:T(8,128)S(1)}, bf16[4,32,2816]{2,1,0:T(8,128)(2,1)S(1)}, s32[2,128]{1,0:T(2,128)S(1)}) custom-call(s32[1]{0:T(128)} %bitcast.shard_ref, s32[1,2048]{1,0:T(1,128)} %starts_ref.3, bf16[256,4096]{1,0:T(8,128)(2,1)} %bitcast.18, bf16[256,2048]{1,0:T(8,128)(2,1)} %bitcast.20, bf16[256,4096]{1,0:T(8,128)(2,1)} %bitcast.19), custom_call_target="tpu_custom_call" | custom-call | tf_op jit(solution)/shard_map/pool/pallas_call | solution.py:506
  3.7 1.5 %collective-permute-start = (bf16[4,32,2816]{2,1,0:T(8,128)(2,1)S(1)}, bf16[4,32,2816]{2,1,0:T(8,128)(2,1)S(1)}, u32[]{:S(2)}, u32[]{:S(2)}) collective-permute-start(bf16[4,32,2816]{2,1,0:T(8,128)(2,1)S(1)} %get-tuple-element.31), channel_id=1, source_target_pairs={{0,1},{1,0},{2,3},{3,2},{4,5},{5,4},{6,7},{7,6},{8,9},{9,8},{10,11... | collective-permute-start | bytes 2162696 | tf_op jit(solution)/shard_map/ppermute | solution.py:525
  5.2 0.0 copy-done
  5.2 0.5 lengths.1.inv_ref
  5.7 1.4 %collective-permute-done.rims_ref = bf16[4,32,2816]{2,1,0:T(8,128)(2,1)S(1)} collective-permute-done((bf16[4,32,2816]{2,1,0:T(8,128)(2,1)S(1)}, bf16[4,32,2816]{2,1,0:T(8,128)(2,1)S(1)}, u32[]{:S(2)}, u32[]{:S(2)}) %collective-permute-start) | collective-permute-done | bytes 720928 | tf_op jit(solution)/shard_map/ppermute | solution.py:525
  7.1 0.3 send.1
  7.4 0.0 copy-start.2
  7.4 32.2 %all_to_all.10.mine_ref = bf16[16,488,128]{2,1,0:T(8,128)(2,1)S(1)} all-to-all(bf16[16,488,128]{2,1,0:T(8,128)(2,1)S(1)} %send.1), channel_id=1, replica_groups={{0,2,4,6,8,10,12,14,16,18,20,22,24,26,28,30},{1,3,5,7,9,11,13,15,17,19,..., dimensions={0} | all-to-all | bytes 3997696 | tf_op jit(solution)/shard_map/all_to_all | solution.py:546
  39.6 0.0 copy-done.2
  39.6 0.3 keys.1
  39.9 2.5 %collective-permute-start.1 = (bf16[16,128,128]{2,1,0:T(8,128)(2,1)S(1)}, bf16[16,128,128]{2,1,0:T(8,128)(2,1)S(1)}, u32[]{:S(2)}, u32[]{:S(2)}) collective-permute-start(bf16[16,128,128]{2,1,0:T(8,128)(2,1)S(1)} %get-tuple-element.36.mine_ref), channel_id=1, source_target_pairs={{0,1},{1,0},{2,3},{3,2},{4,5},{5,4},{6,7},{7,6},{8,9},{9,8},{10,11... | collective-permute-start | bytes 1572872 | tf_op jit(solution)/shard_map/ppermute | solution.py:557
  42.4 0.0 copy-done.1
  42.4 0.5 queries.1
  42.9 1.0 %collective-permute-done.1.other_ref = bf16[16,128,128]{2,1,0:T(8,128)(2,1)S(1)} collective-permute-done((bf16[16,128,128]{2,1,0:T(8,128)(2,1)S(1)}, bf16[16,128,128]{2,1,0:T(8,128)(2,1)S(1)}, u32[]{:S(2)}, u32[]{:S(2)}) %collective-permute-start.1) | collective-permute-done | bytes 524320 | tf_op jit(solution)/shard_map/ppermute | solution.py:557
  44.0 7.9 %attend.1 = (f32[16,128,128]{2,1,0:T(8,128)S(1)}, f32[16,128,128]{2,1,0:T(8,128)S(1)}, bf16[17,128,128]{2,1,0:T(8,128)(2,1)S(1)}, f32[8,128]{1,0:T(8,128)S(1)}) custom-call(s32[1]{0:T(128)} %bitcast.shard_ref, bf16[16,128,128]{2,1,0:T(8,128)(2,1)S(1)} %get-tuple-element.34.query_ref, bf16[16,128,128]{2,1,0:T(8,128)(2,1)S(1)} %get-tuple-element.35.grad_ref, ...), custom_call_target="tpu_custom_call" | custom-call | tf_op jit(solution)/shard_map/attend/pallas_call | solution.py:568
  51.9 0.4 collective-permute-start.2
  52.3 1.7 %collective-permute-start.4 = (f32[8,128]{1,0:T(8,128)S(1)}, f32[8,128]{1,0:T(8,128)S(1)}, u32[]{:S(2)}, u32[]{:S(2)}) collective-permute-start(f32[8,128]{1,0:T(8,128)S(1)} %get-tuple-element.44.gain_ref), channel_id=1, source_target_pairs={{0,33},{1,32},{2,35},{3,34},{4,37},{5,36},{6,39},{7,38},{8,41},{9,... | collective-permute-start | bytes 12296 | tf_op jit(solution)/shard_map/ppermute | solution.py:590
  54.0 0.0 collective-permute-start.3
  54.0 0.5 finish.1
  54.5 0.8 collective-permute-done.4.cross_ref
  55.3 1.1 %collective-permute-done.3.near_ref = f32[8,128]{1,0:T(8,128)S(1)} collective-permute-done((f32[8,128]{1,0:T(8,128)S(1)}, f32[8,128]{1,0:T(8,128)S(1)}, u32[]{:S(2)}, u32[]{:S(2)}) %collective-permute-start.3) | collective-permute-done | bytes 4128 | tf_op jit(solution)/shard_map/ppermute | solution.py:588
  56.5 0.0 collective-permute-done.2.got_ref
  56.5 0.4 merge.1
  56.9 21.3 %all_to_all.11.x_ref = bf16[16,336,128]{2,1,0:T(8,128)(2,1)S(1)} all-to-all(bf16[16,336,128]{2,1,0:T(8,128)(2,1)S(1)} %merge.1), channel_id=1, replica_groups={{0,2,4,6,8,10,12,14,16,18,20,22,24,26,28,30},{1,3,5,7,9,11,13,15,17,19,..., dimensions={0} | all-to-all | bytes 2752512 | tf_op jit(solution)/shard_map/all_to_all | solution.py:608
  78.1 0.3 back.1
  78.4 3.4 %collective-permute-start.5 = (bf16[4,32,1664]{2,1,0:T(8,128)(2,1)S(1)}, bf16[4,32,1664]{2,1,0:T(8,128)(2,1)S(1)}, u32[]{:S(2)}, u32[]{:S(2)}) collective-permute-start(bf16[4,32,1664]{2,1,0:T(8,128)(2,1)S(1)} %get-tuple-element.47), channel_id=1, source_target_pairs={{0,1},{1,0},{2,3},{3,2},{4,5},{5,4},{6,7},{7,6},{8,9},{9,8},{10,11... | collective-permute-start | bytes 1277960 | tf_op jit(solution)/shard_map/ppermute | solution.py:624
  81.8 2.7 %collective-permute-start.6 = (f32[2,128]{1,0:T(2,128)S(1)}, f32[2,128]{1,0:T(2,128)S(1)}, u32[]{:S(2)}, u32[]{:S(2)}) collective-permute-start(f32[2,128]{1,0:T(2,128)S(1)} %get-tuple-element.51), channel_id=1, source_target_pairs={{0,96},{32,64},{64,32},{96,0},{1,97},{33,65},{65,33},{97,1},{2,98}... | collective-permute-start | bytes 3080 | tf_op jit(solution)/shard_map/ppermute | solution.py:625
  84.5 0.0 collective-permute-done.5.rims_ref
  84.5 2.0 %spread.1 = (bf16[256,4096]{1,0:T(8,128)(2,1)}, bf16[256,2048]{1,0:T(8,128)(2,1)}) custom-call(s32[2,128]{1,0:T(2,128)S(1)} %get-tuple-element.29.edges_ref, bf16[4,32,1664]{2,1,0:T(8,128)(2,1)S(1)} %collective-permute-done.5.rims_ref, bf16[4,64,1536]{2,1,0:T(8,128)(2,1)S(1)} %get-tuple-element.48.rows_ref), custom_call_target="tpu_custom_call" | custom-call | tf_op jit(solution)/shard_map/spread/pallas_call | solution.py:626
  86.5 0.0 collective-permute-done.6
  86.5 0.5 slice_bitcast_fusion
  (2 shorter events, 0.0 us)
Async XLA Ops:
  0.6 4.6 %copy-start = (s32[1,2048]{1,0:T(1,128)S(1)}, s32[1,2048]{1,0:T(1,128)}, u32[]{:S(2)}) copy-start(s32[1,2048]{1,0:T(1,128)} %starts_ref.3) | copy-start | bytes 24580
  3.7 3.3 %collective-permute-start = (bf16[4,32,2816]{2,1,0:T(8,128)(2,1)S(1)}, bf16[4,32,2816]{2,1,0:T(8,128)(2,1)S(1)}, u32[]{:S(2)}, u32[]{:S(2)}) collective-permute-start(bf16[4,32,2816]{2,1,0:T(8,128)(2,1)S(1)} %get-tuple-element.31), channel_id=1, source_target_pairs={{0,1},{1,0},{2,3},{3,2},{4,5},{5,4},{6,7},{7,6},{8,9},{9,8},{10,11... | collective-permute-start | bytes 2162696 | tf_op jit(solution)/shard_map/ppermute | solution.py:525
  7.4 32.2 %copy-start.2 = (f32[128]{0:T(128)S(1)}, f32[128]{0:T(128)}, u32[]{:S(2)}) copy-start(f32[128]{0:T(128)} %param.11) | copy-start | bytes 1540
  39.6 2.8 %copy-start.1 = (f32[128]{0:T(128)S(1)}, f32[128]{0:T(128)}, u32[]{:S(2)}) copy-start(f32[128]{0:T(128)} %param.10) | copy-start | bytes 1540
  39.9 4.0 %collective-permute-start.1 = (bf16[16,128,128]{2,1,0:T(8,128)(2,1)S(1)}, bf16[16,128,128]{2,1,0:T(8,128)(2,1)S(1)}, u32[]{:S(2)}, u32[]{:S(2)}) collective-permute-start(bf16[16,128,128]{2,1,0:T(8,128)(2,1)S(1)} %get-tuple-element.36.mine_ref), channel_id=1, source_target_pairs={{0,1},{1,0},{2,3},{3,2},{4,5},{5,4},{6,7},{7,6},{8,9},{9,8},{10,11... | collective-permute-start | bytes 1572872 | tf_op jit(solution)/shard_map/ppermute | solution.py:557
  51.9 4.6 %collective-permute-start.2 = (bf16[17,128,128]{2,1,0:T(8,128)(2,1)S(1)}, bf16[17,128,128]{2,1,0:T(8,128)(2,1)S(1)}, u32[]{:S(2)}, u32[]{:S(2)}) collective-permute-start(bf16[17,128,128]{2,1,0:T(8,128)(2,1)S(1)} %get-tuple-element.43), channel_id=1, source_target_pairs={{0,1},{1,0},{2,3},{3,2},{4,5},{5,4},{6,7},{7,6},{8,9},{9,8},{10,11... | collective-permute-start | bytes 1671176 | tf_op jit(solution)/shard_map/ppermute | solution.py:586
  52.3 3.0 %collective-permute-start.4 = (f32[8,128]{1,0:T(8,128)S(1)}, f32[8,128]{1,0:T(8,128)S(1)}, u32[]{:S(2)}, u32[]{:S(2)}) collective-permute-start(f32[8,128]{1,0:T(8,128)S(1)} %get-tuple-element.44.gain_ref), channel_id=1, source_target_pairs={{0,33},{1,32},{2,35},{3,34},{4,37},{5,36},{6,39},{7,38},{8,41},{9,... | collective-permute-start | bytes 12296 | tf_op jit(solution)/shard_map/ppermute | solution.py:590
  54.0 2.5 %collective-permute-start.3 = (f32[8,128]{1,0:T(8,128)S(1)}, f32[8,128]{1,0:T(8,128)S(1)}, u32[]{:S(2)}, u32[]{:S(2)}) collective-permute-start(f32[8,128]{1,0:T(8,128)S(1)} %get-tuple-element.44.gain_ref), channel_id=1, source_target_pairs={{0,32},{32,0},{64,96},{96,64},{1,33},{33,1},{65,97},{97,65},{2,34}... | collective-permute-start | bytes 12296 | tf_op jit(solution)/shard_map/ppermute | solution.py:588
  78.4 6.1 %collective-permute-start.5 = (bf16[4,32,1664]{2,1,0:T(8,128)(2,1)S(1)}, bf16[4,32,1664]{2,1,0:T(8,128)(2,1)S(1)}, u32[]{:S(2)}, u32[]{:S(2)}) collective-permute-start(bf16[4,32,1664]{2,1,0:T(8,128)(2,1)S(1)} %get-tuple-element.47), channel_id=1, source_target_pairs={{0,1},{1,0},{2,3},{3,2},{4,5},{5,4},{6,7},{7,6},{8,9},{9,8},{10,11... | collective-permute-start | bytes 1277960 | tf_op jit(solution)/shard_map/ppermute | solution.py:624
  81.8 4.7 %collective-permute-start.6 = (f32[2,128]{1,0:T(2,128)S(1)}, f32[2,128]{1,0:T(2,128)S(1)}, u32[]{:S(2)}, u32[]{:S(2)}) collective-permute-start(f32[2,128]{1,0:T(2,128)S(1)} %get-tuple-element.51), channel_id=1, source_target_pairs={{0,96},{32,64},{64,32},{96,0},{1,97},{33,65},{65,33},{97,1},{2,98}... | collective-permute-start | bytes 3080 | tf_op jit(solution)/shard_map/ppermute | solution.py:625
where the time goes:
time: 87.2 us; the launch traced here: 87.1 us
  blocking collectives  53.5 us (61%)
  Pallas kernels  15.8 us (18%)
  starting transfers between devices  12.2 us (14%)
  waiting for transfers between devices  4.3 us (5%)
    all_to_all x1, blocking collectives, shards(): lax.all_to_all(send, 'ctx', 0, 0, tiled=True, axis_index_groups=sides)  32.2 us
    all_to_all x1, blocking collectives, shards(): lax.all_to_all(back, 'ctx', 0, 0, tiled=True, axis_index_groups=sides)  21.3 us
    pallas_call x1, Pallas kernels, shards(): pl.pallas_call(attend_kernel, in_specs=[smem] + [vmem] * 6, out_specs=[vm...  7.92 us
    ppermute x2, starting transfers between devices, shards(): rims = lax.ppermute(rims, 'ctx', mates)  4.94 us
    pallas_call x1, Pallas kernels, shards(): pl.pallas_call(pool_kernel, in_specs=[smem] + [hbm] * 4, out_specs=[vmem]...  3.07 us
    ppermute x1, starting transfers between devices, shards(): lax.ppermute(gains, 'dp', [(i, docs - 1 - i) for i in range(docs)])  2.66 us
    ppermute x1, starting transfers between devices, shards(): other = lax.ppermute(keyval, 'ctx', mates)  2.51 us
    pallas_call x1, Pallas kernels, shards(): pl.pallas_call(spread_kernel, in_specs=[vmem] * 3, out_specs=[hbm] * 2, o...  2 us
  transfers between devices with their start and end apart: 7, of which 4 were waited for; matrix products, arithmetic and copies ran while one was open for 0% of the time, Pallas kernels for 4%

commit v1 on v0

--- a/solution.py
+++ b/solution.py
@@ -223,8 +223,6 @@
     grad_ref,
     mine_ref,
     other_ref,
-    qgain_ref,
-    kgain_ref,
     dq_ref,
     keep_ref,
     give_ref,
@@ -334,12 +332,9 @@
             inv_sum = 1.0 / jnp.sum(sums[0], axis=0, keepdims=True)
             stats = (inv_sum, jnp.sum(sums[1], axis=0, keepdims=True) * inv_sum)
 
-    key_total = jnp.zeros((1, head), f32)
     for n in range(patches // key_blk):
         at = pl.ds(n * key_blk, key_blk)
-        dk = dk_ref[at, :] * scaling
-        dk_ref[at, :] = dk
-        key_total = key_total + jnp.sum(dk * key_ref[at, :].astype(f32), axis=0, keepdims=True)
+        dk_ref[at, :] = dk_ref[at, :] * scaling
 
     for c in range(chips):
         mine, theirs = places(c)
@@ -347,8 +342,7 @@
         keep_ref[c, own:, :] = dv_ref[mine, :]
         give_ref[c, :own, :] = dk_ref[theirs, :].astype(bf16)
         give_ref[c, own:, :] = dv_ref[theirs, :].astype(bf16)
-    gains = jnp.concatenate([total / qgain_ref[...], key_total / kgain_ref[...]], axis=0)
-    parts = in_parts(gains)
+    parts = in_parts(total)
     gain_ref[...] = parts
     give_ref[chips] = jnp.concatenate([parts, jnp.zeros((lanes - extra, head), f32)], axis=0).astype(bf16)
 
@@ -357,11 +351,11 @@
     high = gains.astype(bf16).astype(f32)
     middle = (gains - high).astype(bf16).astype(f32)
     low = (gains - high - middle).astype(bf16).astype(f32)
-    return jnp.concatenate([high, middle, low, jnp.zeros((extra - 6, head), f32)], axis=0)
+    return jnp.concatenate([high, middle, low, jnp.zeros((extra - 3, head), f32)], axis=0)
 
 
 def joined(parts):
-    return parts[0:2] + parts[2:4] + parts[4:6]
+    return parts[0:1] + parts[1:2] + parts[2:3]
 
 
 def norm_back(delta, gain, unit, scale):
@@ -384,7 +378,7 @@
     chips, own, _ = inv_ref.shape
     even = is_even(shard_ref)
     here = joined(gain_ref[...]) + joined(got_ref[chips].astype(f32))
-    tail = in_parts(here + (joined(near_ref[...]) + joined(cross_ref[...])))[:6]
+    tail = in_parts(here + (joined(near_ref[...]) + joined(cross_ref[...])))[:3]
     for c in range(chips):
         kept = keep_ref[c] + got_ref[c].astype(f32)
         keys = norm_back(kept[:own], kgain_ref[...], kunit_ref[c], kscale_ref[c])
@@ -405,11 +399,11 @@
             at = 4 * own + part * edge
             out_ref[c, at : at + edge, :] = jnp.where(even, above, below).astype(bf16)
             lones.append(lone[edge - 1 :])
-        last = jnp.concatenate([tail] + lones + [none[: edge - 10]], axis=0)
+        last = jnp.concatenate([tail] + lones + [none[: extra - 7]], axis=0)
         out_ref[c, 4 * (own + edge) :, :] = last.astype(bf16)
 
 
-def back_kernel(shard_ref, x_ref, rows_ref, rims_ref, gain_ref):
+def back_kernel(shard_ref, x_ref, qgain_ref, kgain_ref, rows_ref, rims_ref, gain_ref):
     chips = x_ref.shape[0]
     chunks, own, width = rows_ref.shape
     per = 2 * chips // chunks
@@ -423,7 +417,7 @@
         return (
             x_ref[chip, part * own : (part + 1) * own, :].astype(f32),
             x_ref[chip, at : at + edge, :].astype(f32),
-            ends[6 + part : 7 + part],
+            ends[3 + part : 4 + part],
         )
 
     def keyval_pieces(n):
@@ -448,7 +442,8 @@
     tail = x_ref[0, 4 * (own + edge) :, :].astype(f32)
     for c in range(1, chips):
         tail = tail + x_ref[c, 4 * (own + edge) :, :].astype(f32)
-    gain_ref[...] = joined(tail)
+    gain_ref[0:1, :] = joined(tail) / qgain_ref[...]
+    gain_ref[1:2, :] = joined(tail) / kgain_ref[...]
 
 
 def spread_kernel(edges_ref, rims_ref, rows_ref, query_ref, keyval_ref, query_buf, keyval_buf, sems):
@@ -567,7 +562,7 @@
     block = (patches, head)
     dq, keep, give, gains = pl.pallas_call(
         attend_kernel,
-        in_specs=[smem] + [vmem] * 6,
+        in_specs=[smem] + [vmem] * 4,
         out_specs=[vmem] * 4,
         out_shape=[
             shape(f32, *pair),
@@ -582,7 +577,7 @@
         + [pltpu.VMEM((head, query_blk), f32)],
         compiler_params=limit(36),
         name="attend",
-    )(which, query, grad, keyval, other, qgain, kgain)
+    )(which, query, grad, keyval, other)
     got = lax.ppermute(give, "ctx", mates)
     docs = lax.axis_size("dp")
     near = lax.ppermute(gains, "dp", [(i, i ^ 1) for i in range(docs)])
@@ -601,7 +596,7 @@
         merge_kernel,
         in_specs=[smem] + [vmem] * 10,
         out_specs=vmem,
-        out_shape=shape(bf16, chips, 4 * (own + edge) + edge, head),
+        out_shape=shape(bf16, chips, 4 * (own + edge) + extra, head),
         compiler_params=limit(16),
         name="merge",
     )(which, rows, keep, got, gains, near, cross, kunit, kscale, inv_len, kgain)
@@ -611,7 +606,7 @@
     wide = qcols + vcols + head
     rows, rims, gains = pl.pallas_call(
         back_kernel,
-        in_specs=[smem, vmem],
+        in_specs=[smem] + [vmem] * 3,
         out_specs=[vmem] * 3,
         out_shape=[
             shape(bf16, chunks, own, qcols + vcols),
@@ -620,7 +615,7 @@
         ],
         compiler_params=limit(32),
         name="back",
-    )(which, home)
+    )(which, home, qgain, kgain)
     rims = lax.ppermute(rims, "ctx", mates)
     opposite = lax.ppermute(gains, "dp", [(i, docs - 1 - i) for i in range(docs)])
     query_out, keyval_out = pl.pallas_call(

time: 87.2 us -> 87 us (level)
  no operation moved by 1% of the time
where the time goes in v1:
time: 87 us; the launch traced here: 86.8 us
  blocking collectives  53 us (61%)
  Pallas kernels  15.8 us (18%)
  starting transfers between devices  12.4 us (14%)
  waiting for transfers between devices  4.29 us (5%)
    all_to_all x1, blocking collectives, shards(): lax.all_to_all(send, 'ctx', 0, 0, tiled=True, axis_index_groups=sides)  32.2 us
    all_to_all x1, blocking collectives, shards(): lax.all_to_all(back, 'ctx', 0, 0, tiled=True, axis_index_groups=sides)  20.8 us
    pallas_call x1, Pallas kernels, shards(): pl.pallas_call(attend_kernel, in_specs=[smem] + [vmem] * 4, out_specs=[vm...  7.98 us
    ppermute x2, starting transfers between devices, shards(): rims = lax.ppermute(rims, 'ctx', mates)  5.1 us
    pallas_call x1, Pallas kernels, shards(): pl.pallas_call(pool_kernel, in_specs=[smem] + [hbm] * 4, out_specs=[vmem]...  3.07 us
    ppermute x1, starting transfers between devices, shards(): lax.ppermute(gains, 'dp', [(i, docs - 1 - i) for i in range(docs)])  2.66 us
    ppermute x1, starting transfers between devices, shards(): other = lax.ppermute(keyval, 'ctx', mates)  2.51 us
    pallas_call x1, Pallas kernels, shards(): pl.pallas_call(spread_kernel, in_specs=[vmem] * 3, out_specs=[hbm] * 2, o...  2.01 us
  transfers between devices with their start and end apart: 7, of which 4 were waited for; matrix products, arithmetic and copies ran while one was open for 0% of the time, Pallas kernels for 4%

profile of v1, /device:TPU:1, one launch (start us, length us, event | category | flops | bytes accessed | tf_op | source)
XLA Modules:
  0.0 86.8 jit_solution(15403554026216703163)
XLA Ops:
  0.6 0.0 copy-start
  0.6 3.1 %pool.1 = (f32[4,64,2560]{2,1,0:T(8,128)S(1)}, bf16[4,32,2816]{2,1,0:T(8,128)(2,1)S(1)}, s32[2,128]{1,0:T(2,128)S(1)}) custom-call(s32[1]{0:T(128)} %bitcast.shard_ref, s32[1,2048]{1,0:T(1,128)} %starts_ref.3, bf16[256,4096]{1,0:T(8,128)(2,1)} %bitcast.18, bf16[256,2048]{1,0:T(8,128)(2,1)} %bitcast.20, bf16[256,4096]{1,0:T(8,128)(2,1)} %bitcast.19), custom_call_target="tpu_custom_call" | custom-call | tf_op jit(solution)/shard_map/pool/pallas_call | solution.py:501
  3.7 1.5 %collective-permute-start = (bf16[4,32,2816]{2,1,0:T(8,128)(2,1)S(1)}, bf16[4,32,2816]{2,1,0:T(8,128)(2,1)S(1)}, u32[]{:S(2)}, u32[]{:S(2)}) collective-permute-start(bf16[4,32,2816]{2,1,0:T(8,128)(2,1)S(1)} %get-tuple-element.31), channel_id=1, source_target_pairs={{0,1},{1,0},{2,3},{3,2},{4,5},{5,4},{6,7},{7,6},{8,9},{9,8},{10,11... | collective-permute-start | bytes 2162696 | tf_op jit(solution)/shard_map/ppermute | solution.py:520
  5.2 0.0 copy-done
  5.2 0.5 lengths.1.inv_ref
  5.7 1.4 %collective-permute-done.rims_ref = bf16[4,32,2816]{2,1,0:T(8,128)(2,1)S(1)} collective-permute-done((bf16[4,32,2816]{2,1,0:T(8,128)(2,1)S(1)}, bf16[4,32,2816]{2,1,0:T(8,128)(2,1)S(1)}, u32[]{:S(2)}, u32[]{:S(2)}) %collective-permute-start) | collective-permute-done | bytes 720928 | tf_op jit(solution)/shard_map/ppermute | solution.py:520
  7.1 0.3 send.1
  7.4 0.0 copy-start.2
  7.4 32.2 %all_to_all.10.mine_ref = bf16[16,488,128]{2,1,0:T(8,128)(2,1)S(1)} all-to-all(bf16[16,488,128]{2,1,0:T(8,128)(2,1)S(1)} %send.1), channel_id=1, replica_groups={{0,2,4,6,8,10,12,14,16,18,20,22,24,26,28,30},{1,3,5,7,9,11,13,15,17,19,..., dimensions={0} | all-to-all | bytes 3997696 | tf_op jit(solution)/shard_map/all_to_all | solution.py:541
  39.6 0.0 copy-done.2
  39.6 0.3 keys.1
  39.9 2.5 %collective-permute-start.1 = (bf16[16,128,128]{2,1,0:T(8,128)(2,1)S(1)}, bf16[16,128,128]{2,1,0:T(8,128)(2,1)S(1)}, u32[]{:S(2)}, u32[]{:S(2)}) collective-permute-start(bf16[16,128,128]{2,1,0:T(8,128)(2,1)S(1)} %get-tuple-element.36.mine_ref), channel_id=1, source_target_pairs={{0,1},{1,0},{2,3},{3,2},{4,5},{5,4},{6,7},{7,6},{8,9},{9,8},{10,11... | collective-permute-start | bytes 1572872 | tf_op jit(solution)/shard_map/ppermute | solution.py:552
  42.4 0.0 copy-done.1
  42.4 0.5 queries.1
  42.9 1.0 %collective-permute-done.1.other_ref = bf16[16,128,128]{2,1,0:T(8,128)(2,1)S(1)} collective-permute-done((bf16[16,128,128]{2,1,0:T(8,128)(2,1)S(1)}, bf16[16,128,128]{2,1,0:T(8,128)(2,1)S(1)}, u32[]{:S(2)}, u32[]{:S(2)}) %collective-permute-start.1) | collective-permute-done | bytes 524320 | tf_op jit(solution)/shard_map/ppermute | solution.py:552
  43.9 8.0 %attend.1 = (f32[16,128,128]{2,1,0:T(8,128)S(1)}, f32[16,128,128]{2,1,0:T(8,128)S(1)}, bf16[17,128,128]{2,1,0:T(8,128)(2,1)S(1)}, f32[8,128]{1,0:T(8,128)S(1)}) custom-call(s32[1]{0:T(128)} %bitcast.shard_ref, bf16[16,128,128]{2,1,0:T(8,128)(2,1)S(1)} %get-tuple-element.34.query_ref, bf16[16,128,128]{2,1,0:T(8,128)(2,1)S(1)} %get-tuple-element.35.grad_ref, ...), custom_call_target="tpu_custom_call" | custom-call | tf_op jit(solution)/shard_map/attend/pallas_call | solution.py:563
  51.9 0.4 collective-permute-start.2
  52.4 1.7 %collective-permute-start.4 = (f32[8,128]{1,0:T(8,128)S(1)}, f32[8,128]{1,0:T(8,128)S(1)}, u32[]{:S(2)}, u32[]{:S(2)}) collective-permute-start(f32[8,128]{1,0:T(8,128)S(1)} %get-tuple-element.44.gain_ref), channel_id=1, source_target_pairs={{0,33},{1,32},{2,35},{3,34},{4,37},{5,36},{6,39},{7,38},{8,41},{9,... | collective-permute-start | bytes 12296 | tf_op jit(solution)/shard_map/ppermute | solution.py:585
  54.1 0.0 collective-permute-start.3
  54.1 0.5 finish.1
  54.6 0.8 collective-permute-done.4.cross_ref
  55.4 1.1 %collective-permute-done.3.near_ref = f32[8,128]{1,0:T(8,128)S(1)} collective-permute-done((f32[8,128]{1,0:T(8,128)S(1)}, f32[8,128]{1,0:T(8,128)S(1)}, u32[]{:S(2)}, u32[]{:S(2)}) %collective-permute-start.3) | collective-permute-done | bytes 4128 | tf_op jit(solution)/shard_map/ppermute | solution.py:583
  56.5 0.0 collective-permute-done.2.got_ref
  56.5 0.4 merge.1
  56.9 20.8 %all_to_all.11.x_ref = bf16[16,328,128]{2,1,0:T(8,128)(2,1)S(1)} all-to-all(bf16[16,328,128]{2,1,0:T(8,128)(2,1)S(1)} %merge.1), channel_id=1, replica_groups={{0,2,4,6,8,10,12,14,16,18,20,22,24,26,28,30},{1,3,5,7,9,11,13,15,17,19,..., dimensions={0} | all-to-all | bytes 2686976 | tf_op jit(solution)/shard_map/all_to_all | solution.py:603
  77.7 0.3 back.1
  78.0 3.6 %collective-permute-start.5 = (bf16[4,32,1664]{2,1,0:T(8,128)(2,1)S(1)}, bf16[4,32,1664]{2,1,0:T(8,128)(2,1)S(1)}, u32[]{:S(2)}, u32[]{:S(2)}) collective-permute-start(bf16[4,32,1664]{2,1,0:T(8,128)(2,1)S(1)} %get-tuple-element.47), channel_id=1, source_target_pairs={{0,1},{1,0},{2,3},{3,2},{4,5},{5,4},{6,7},{7,6},{8,9},{9,8},{10,11... | collective-permute-start | bytes 1277960 | tf_op jit(solution)/shard_map/ppermute | solution.py:619
  81.5 2.7 %collective-permute-start.6 = (f32[2,128]{1,0:T(2,128)S(1)}, f32[2,128]{1,0:T(2,128)S(1)}, u32[]{:S(2)}, u32[]{:S(2)}) collective-permute-start(f32[2,128]{1,0:T(2,128)S(1)} %get-tuple-element.51), channel_id=1, source_target_pairs={{0,96},{32,64},{64,32},{96,0},{1,97},{33,65},{65,33},{97,1},{2,98}... | collective-permute-start | bytes 3080 | tf_op jit(solution)/shard_map/ppermute | solution.py:620
  84.2 0.0 collective-permute-done.5.rims_ref
  84.2 2.0 %spread.1 = (bf16[256,4096]{1,0:T(8,128)(2,1)}, bf16[256,2048]{1,0:T(8,128)(2,1)}) custom-call(s32[2,128]{1,0:T(2,128)S(1)} %get-tuple-element.29.edges_ref, bf16[4,32,1664]{2,1,0:T(8,128)(2,1)S(1)} %collective-permute-done.5.rims_ref, bf16[4,64,1536]{2,1,0:T(8,128)(2,1)S(1)} %get-tuple-element.48.rows_ref), custom_call_target="tpu_custom_call" | custom-call | tf_op jit(solution)/shard_map/spread/pallas_call | solution.py:621
  86.2 0.0 collective-permute-done.6
  86.2 0.5 slice_bitcast_fusion
  (2 shorter events, 0.0 us)
Async XLA Ops:
  0.6 4.6 %copy-start = (s32[1,2048]{1,0:T(1,128)S(1)}, s32[1,2048]{1,0:T(1,128)}, u32[]{:S(2)}) copy-start(s32[1,2048]{1,0:T(1,128)} %starts_ref.3) | copy-start | bytes 24580
  3.7 3.3 %collective-permute-start = (bf16[4,32,2816]{2,1,0:T(8,128)(2,1)S(1)}, bf16[4,32,2816]{2,1,0:T(8,128)(2,1)S(1)}, u32[]{:S(2)}, u32[]{:S(2)}) collective-permute-start(bf16[4,32,2816]{2,1,0:T(8,128)(2,1)S(1)} %get-tuple-element.31), channel_id=1, source_target_pairs={{0,1},{1,0},{2,3},{3,2},{4,5},{5,4},{6,7},{7,6},{8,9},{9,8},{10,11... | collective-permute-start | bytes 2162696 | tf_op jit(solution)/shard_map/ppermute | solution.py:520
  7.4 32.2 %copy-start.2 = (f32[128]{0:T(128)S(1)}, f32[128]{0:T(128)}, u32[]{:S(2)}) copy-start(f32[128]{0:T(128)} %param.11) | copy-start | bytes 1540
  39.6 2.8 %copy-start.1 = (f32[128]{0:T(128)S(1)}, f32[128]{0:T(128)}, u32[]{:S(2)}) copy-start(f32[128]{0:T(128)} %param.10) | copy-start | bytes 1540
  39.9 4.0 %collective-permute-start.1 = (bf16[16,128,128]{2,1,0:T(8,128)(2,1)S(1)}, bf16[16,128,128]{2,1,0:T(8,128)(2,1)S(1)}, u32[]{:S(2)}, u32[]{:S(2)}) collective-permute-start(bf16[16,128,128]{2,1,0:T(8,128)(2,1)S(1)} %get-tuple-element.36.mine_ref), channel_id=1, source_target_pairs={{0,1},{1,0},{2,3},{3,2},{4,5},{5,4},{6,7},{7,6},{8,9},{9,8},{10,11... | collective-permute-start | bytes 1572872 | tf_op jit(solution)/shard_map/ppermute | solution.py:552
  51.9 4.6 %collective-permute-start.2 = (bf16[17,128,128]{2,1,0:T(8,128)(2,1)S(1)}, bf16[17,128,128]{2,1,0:T(8,128)(2,1)S(1)}, u32[]{:S(2)}, u32[]{:S(2)}) collective-permute-start(bf16[17,128,128]{2,1,0:T(8,128)(2,1)S(1)} %get-tuple-element.43), channel_id=1, source_target_pairs={{0,1},{1,0},{2,3},{3,2},{4,5},{5,4},{6,7},{7,6},{8,9},{9,8},{10,11... | collective-permute-start | bytes 1671176 | tf_op jit(solution)/shard_map/ppermute | solution.py:581
  52.4 3.0 %collective-permute-start.4 = (f32[8,128]{1,0:T(8,128)S(1)}, f32[8,128]{1,0:T(8,128)S(1)}, u32[]{:S(2)}, u32[]{:S(2)}) collective-permute-start(f32[8,128]{1,0:T(8,128)S(1)} %get-tuple-element.44.gain_ref), channel_id=1, source_target_pairs={{0,33},{1,32},{2,35},{3,34},{4,37},{5,36},{6,39},{7,38},{8,41},{9,... | collective-permute-start | bytes 12296 | tf_op jit(solution)/shard_map/ppermute | solution.py:585
  54.1 2.5 %collective-permute-start.3 = (f32[8,128]{1,0:T(8,128)S(1)}, f32[8,128]{1,0:T(8,128)S(1)}, u32[]{:S(2)}, u32[]{:S(2)}) collective-permute-start(f32[8,128]{1,0:T(8,128)S(1)} %get-tuple-element.44.gain_ref), channel_id=1, source_target_pairs={{0,32},{32,0},{64,96},{96,64},{1,33},{33,1},{65,97},{97,65},{2,34}... | collective-permute-start | bytes 12296 | tf_op jit(solution)/shard_map/ppermute | solution.py:583
  78.0 6.3 %collective-permute-start.5 = (bf16[4,32,1664]{2,1,0:T(8,128)(2,1)S(1)}, bf16[4,32,1664]{2,1,0:T(8,128)(2,1)S(1)}, u32[]{:S(2)}, u32[]{:S(2)}) collective-permute-start(bf16[4,32,1664]{2,1,0:T(8,128)(2,1)S(1)} %get-tuple-element.47), channel_id=1, source_target_pairs={{0,1},{1,0},{2,3},{3,2},{4,5},{5,4},{6,7},{7,6},{8,9},{9,8},{10,11... | collective-permute-start | bytes 1277960 | tf_op jit(solution)/shard_map/ppermute | solution.py:619
  81.5 4.7 %collective-permute-start.6 = (f32[2,128]{1,0:T(2,128)S(1)}, f32[2,128]{1,0:T(2,128)S(1)}, u32[]{:S(2)}, u32[]{:S(2)}) collective-permute-start(f32[2,128]{1,0:T(2,128)S(1)} %get-tuple-element.51), channel_id=1, source_target_pairs={{0,96},{32,64},{64,32},{96,0},{1,97},{33,65},{65,33},{97,1},{2,98}... | collective-permute-start | bytes 3080 | tf_op jit(solution)/shard_map/ppermute | solution.py:620
